TPU v7x, 512 devices: a whole 4x4x16 slice. The times are simulated.
512 devices in a mesh: sect: 8 (over z_hi, core), dom: 64 (over y, x, z_lo).
Axes of the slice: x: 4, y: 4, z: 16 (z_hi: 4, z_lo: 4; z = z_hi * 4 + z_lo), core: 2. Of those that a mesh axis runs over, the one named last changes fastest.
Arguments:
- nodes: bfloat16 [524288, 512], P(('sect', 'dom')), may hold values from -6 to 6
- fine_tiles: bfloat16 [12288, 128, 128], P(('sect', 'dom')), may hold values from -0.3125 to 0.3125
- fine_target: int32 [12288], P(('sect', 'dom')), may hold values from 0 to 7
- fine_source: int32 [12288], P(('sect', 'dom')), may hold values from 0 to 11
- halo_ids: int32 [512, 2, 2], P(('sect', 'dom')), may hold values from 0 to 7
- pool_map: int32 [4096], P(('sect', 'dom')), may hold values from 0 to 5, as said below
- pool_weight: bfloat16 [524288], P(('sect', 'dom')), may hold values from 0.099609375 to 1
- coarse_tiles: bfloat16 [3072, 128, 128], P(('sect', 'dom')), may hold values from -0.3125 to 0.3125
- coarse_target: int32 [3072], P(('sect', 'dom')), may hold values from 0 to 1
- coarse_source: int32 [3072], P(('sect', 'dom')), may hold values from 0 to 5
- weights: bfloat16 [7, 512, 512], P(None, 'dom'), may hold values from -0.25 to 0.25
Outputs:
- fine_out: bfloat16 [524288, 512], P(('sect', 'dom'))
Inputs may be any that keep to these rules, and one draw needn't show every extreme that they name: `pool_map`: at most 2 fine blocks of a partition pool into the previous partition and at most 2 into the next; none pool across the ends of a section's chain.
All inputs are finite; a program needn't handle non-finite values.
Results may differ from a plain program's by a relative error of at most 0.019.
Values may be sent and summed in bfloat16 or wider, within the bound.
No kernel may reach another device: no remote copies, remote signals or barrier semaphores. Data moves between devices by JAX's collectives and lax.ppermute only.
A program may use at most 64 MiB of HBM per device.

v0:
```python
import jax
import jax.numpy as jnp
from jax import lax
from jax.sharding import PartitionSpec as P

ROUNDS = 2


def with_halo(block, sides, width):
    for axis, dim in sides:
        count = lax.axis_size(axis)
        forward = [(i, i + 1) for i in range(count - 1)]
        backward = [(target, source) for source, target in forward]
        low = lax.ppermute(
            lax.slice_in_dim(block, block.shape[dim] - width, None, axis=dim), axis, forward
        )
        high = lax.ppermute(lax.slice_in_dim(block, 0, width, axis=dim), axis, backward)
        block = jnp.concatenate([low, block, high], axis=dim)
    return block


def aggregate(proj_all, tiles, target, source, count):
    total = jnp.zeros((count,) + proj_all.shape[1:], jnp.float32)

    def add_tile(index, total):
        block = lax.dynamic_index_in_dim(proj_all, source[index], 0, keepdims=False)
        tile = lax.dynamic_index_in_dim(tiles, index, 0, keepdims=False)
        message = jnp.dot(tile, block, preferred_element_type=jnp.float32)
        current = lax.dynamic_index_in_dim(total, target[index], 0, keepdims=False)
        return lax.dynamic_update_index_in_dim(total, current + message, target[index], 0)

    total = lax.fori_loop(0, tiles.shape[0], add_tile, total)
    return total.astype(jnp.bfloat16)


def pool_into(skipped, pool_weight, slot_index, keep, slots):
    count, edge, width = skipped.shape
    weight_rows = pool_weight.reshape(count, edge, 1)
    total = jnp.zeros((slots, edge, width), jnp.float32)

    def add_block(index, total):
        block = lax.dynamic_index_in_dim(skipped, index, 0, keepdims=False).astype(jnp.float32)
        scale = lax.dynamic_index_in_dim(weight_rows, index, 0, keepdims=False).astype(jnp.float32)
        term = jnp.where(keep[index], block * scale, 0.0)
        current = lax.dynamic_index_in_dim(total, slot_index[index], 0, keepdims=False)
        return lax.dynamic_update_index_in_dim(total, current + term, slot_index[index], 0)

    return lax.fori_loop(0, count, add_block, total)


def advance(blocks, summed, own_weight, near_weight):
    width = blocks.shape[-1]
    flat = blocks.reshape(-1, width)
    mixed = jnp.dot(flat, own_weight, preferred_element_type=jnp.float32) + jnp.dot(
        summed.reshape(-1, width), near_weight, preferred_element_type=jnp.float32
    )
    return (
        (flat.astype(jnp.float32) + jax.nn.silu(mixed)).astype(jnp.bfloat16).reshape(blocks.shape)
    )


def on_device(
    nodes,
    fine_tiles,
    fine_target,
    fine_source,
    halo_ids,
    pool_map,
    pool_weight,
    coarse_tiles,
    coarse_target,
    coarse_source,
    weights,
):
    matrices = lax.all_gather(weights, "dom", axis=1, tiled=True)
    width = nodes.shape[1]
    edge = fine_tiles.shape[-1]
    blocks = nodes.reshape(-1, edge, width)
    count = blocks.shape[0]
    groups = count // 4
    outgoing = halo_ids.reshape(-1)
    margin = halo_ids.shape[-1] * edge
    for turn in range(ROUNDS):
        owned = jnp.dot(
            blocks.reshape(-1, width), matrices[0], preferred_element_type=jnp.float32
        ).astype(jnp.bfloat16)
        sent = owned.reshape(-1, edge, width)[outgoing].reshape(-1, width)
        padded = with_halo(sent, ((("sect", "dom"), 0),), margin)
        projected = jnp.concatenate(
            [owned, padded[:margin], padded[padded.shape[0] - margin :]]
        ).reshape(-1, edge, width)
        summed = aggregate(projected, fine_tiles, fine_target, fine_source, count)
        blocks = advance(blocks, summed, matrices[1], matrices[2])
    span = groups * edge
    every_row = pool_map >= 0
    shares = pool_into(blocks, pool_weight, pool_map, every_row, 3 * groups)
    leaving = jnp.concatenate([shares[:groups], shares[2 * groups :]]).reshape(-1, width)
    arrived = with_halo(leaving.astype(jnp.bfloat16), (("dom", 0),), span).astype(leaving.dtype)
    coarse = (
        shares[groups : 2 * groups].reshape(-1, width)
        + arrived[:span]
        + arrived[arrived.shape[0] - span :]
    )
    coarse = coarse.astype(jnp.bfloat16).reshape(groups, edge, width)
    for turn in range(ROUNDS):
        owned = jnp.dot(
            coarse.reshape(-1, width), matrices[3], preferred_element_type=jnp.float32
        ).astype(jnp.bfloat16)
        beside_all = with_halo(owned, (("dom", 0),), span)
        summed = aggregate(
            beside_all.reshape(-1, edge, width), coarse_tiles, coarse_target, coarse_source, groups
        )
        coarse = advance(coarse, summed, matrices[4], matrices[5])
    final_blocks = with_halo(coarse.reshape(-1, width), (("dom", 0),), span)
    lifted = final_blocks.reshape(-1, edge, width)[pool_map]
    result = blocks.reshape(-1, width).astype(jnp.float32) + jnp.dot(
        lifted.reshape(-1, width), matrices[6], preferred_element_type=jnp.float32
    )
    return result.astype(jnp.bfloat16)


def solution(mesh):
    return jax.shard_map(
        on_device,
        mesh=mesh,
        in_specs=(
            P(("sect", "dom"), None),
            P(("sect", "dom"), None, None),
            P(("sect", "dom")),
            P(("sect", "dom")),
            P(("sect", "dom"), None, None),
            P(("sect", "dom")),
            P(("sect", "dom")),
            P(("sect", "dom"), None, None),
            P(("sect", "dom")),
            P(("sect", "dom")),
            P(None, "dom", None),
        ),
        out_specs=P(("sect", "dom"), None),
        check_vma=False,
    )
```

profile of v0, /device:TPU:187, one launch (start us, length us, event | category | flops | bytes accessed | tf_op | source)
XLA Modules:
  0.0 915.9 jit_solution(14589787657087487114)
XLA Ops:
  8.7 303.6 %all-gather.2.cloned.1.call-done = bf16[7,512,512]{2,1,0:T(8,128)(2,1)} async-done(((bf16[7,8,512]{2,1,0:T(8,128)(2,1)}), bf16[7,512,512]{2,1,0:T(8,128)(2,1)}) %all-gather.2.cloned.1.call-update) | async-done | bytes 3670032 | tf_op jit(solution)/shard_map/all_gather | solution.py:75
  312.3 2.1 convolution_convert_fusion.1
  315.0 3.8 collective-permute-start
  318.9 1.9 collective-permute-start.1
  320.8 3.1 fusion.33
  323.9 2.1 collective-permute-done
  328.0 157.4 %while.65 = (s32[]{:T(128)}, f32[8,128,512]{2,1,0:T(8,128)S(1)}, s32[24]{0:T(128)S(1)}, bf16[24,128,128]{2,1,0:T(8,128)(2,1)}, s32[24]{0:T(128)S(1)}, /*index=5*...) while((s32[]{:T(128)}, f32[8,128,512]{2,1,0:T(8,128)S(1)}, s32[24]{0:T(128)S(1)}, ...), condition=%wide.region_1.2_spmd, body=%wide.region_0.1_spmd.sunk | while | flops 16842760 | bytes 1213133 | solution.py:32
  487.1 2.1 add_convert_fusion.2
  489.2 2.1 convolution_convert_fusion
  492.0 8.9 collective-permute-start.2
  500.9 1.9 collective-permute-start.3
  502.9 3.1 fusion.32
  505.9 6.2 collective-permute-done.3
  513.7 149.3 %while.66 = (s32[]{:T(128)}, f32[8,128,512]{2,1,0:T(8,128)S(1)}, s32[24]{0:T(128)S(1)}, bf16[24,128,128]{2,1,0:T(8,128)(2,1)}, s32[24]{0:T(128)S(1)}, /*index=5*...) while((s32[]{:T(128)}, f32[8,128,512]{2,1,0:T(8,128)S(1)}, s32[24]{0:T(128)S(1)}, ...), condition=%wide.region_3.4_spmd, body=%wide.region_2.3_spmd.sunk | while | flops 16842760 | bytes 1213133 | solution.py:32
  664.5 2.1 add_convert_fusion.1
  666.9 36.6 %while.67 = (s32[]{:T(128)}, f32[6,128,512]{2,1,0:T(8,128)S(1)}, s32[8]{0:T(128)S(1)}, pred[8]{0:T(512)(128)(4,1)S(1)}, bf16[8,128,512]{2,1,0:T(8,128)(2,1)S(1)}...) while((s32[]{:T(128)}, f32[6,128,512]{2,1,0:T(8,128)S(1)}, s32[8]{0:T(128)S(1)}, ...), condition=%wide.region_5.6_spmd, body=%wide.region_4.5_spmd.sunk | while | flops 262277 | bytes 656798 | solution.py:48
  703.6 2.3 collective-permute-start.4
  705.9 3.0 collective-permute-start.5
  709.0 1.7 collective-permute-done.4
  710.7 4.2 collective-permute-done.5
  716.4 10.5 %collective-permute-start.6 = (bf16[256,512]{1,0:T(8,128)(2,1)S(1)}, bf16[256,512]{1,0:T(8,128)(2,1)S(1)}, u32[]{:S(2)}, u32[]{:S(2)}) collective-permute-start(bf16[256,512]{1,0:T(8,128)(2,1)S(1)} %convolution_convert_fusion.3), channel_id=1, source_target_pairs={{0,1},{1,2},{2,3},{3,4},{4,5},{5,6},{6,7},{7,8},{8,9},{9,10},{10,1... | collective-permute-start | bytes 786440 | tf_op jit(solution)/shard_map/ppermute | solution.py:14
  726.9 1.9 collective-permute-start.7
  730.2 6.3 collective-permute-done.7
  736.6 35.3 %while.68 = (s32[]{:T(128)}, f32[2,128,512]{2,1,0:T(8,128)S(1)}, s32[6]{0:T(128)S(1)}, bf16[6,128,128]{2,1,0:T(8,128)(2,1)}, s32[6]{0:T(128)S(1)}, /*index=5*/bf...) while((s32[]{:T(128)}, f32[2,128,512]{2,1,0:T(8,128)S(1)}, s32[6]{0:T(128)S(1)}, ...), condition=%wide.region_7.8_spmd, body=%wide.region_6.7_spmd.sunk | while | flops 16842760 | bytes 1213133 | solution.py:32
  774.8 2.7 collective-permute-start.8
  777.5 2.6 collective-permute-start.9
  782.2 3.7 collective-permute-done.9
  786.0 35.3 %while.69 = (s32[]{:T(128)}, f32[2,128,512]{2,1,0:T(8,128)S(1)}, s32[6]{0:T(128)S(1)}, bf16[6,128,128]{2,1,0:T(8,128)(2,1)}, s32[6]{0:T(128)S(1)}, /*index=5*/bf...) while((s32[]{:T(128)}, f32[2,128,512]{2,1,0:T(8,128)S(1)}, s32[6]{0:T(128)S(1)}, ...), condition=%wide.region_9.10_spmd, body=%wide.region_8.9_spmd.sunk | while | flops 16842760 | bytes 1213133 | solution.py:32
  822.8 44.8 %collective-permute-start.10 = (bf16[256,512]{1,0:T(8,128)(2,1)S(1)}, bf16[256,512]{1,0:T(8,128)(2,1)S(1)}, u32[]{:S(2)}, u32[]{:S(2)}) collective-permute-start(bf16[256,512]{1,0:T(8,128)(2,1)S(1)} %add_convert_fusion.3), channel_id=1, source_target_pairs={{0,1},{1,2},{2,3},{3,4},{4,5},{5,6},{6,7},{7,8},{8,9},{9,10},{10,1... | collective-permute-start | bytes 786440 | tf_op jit(solution)/shard_map/ppermute | solution.py:14
  867.6 1.9 collective-permute-start.11
  870.9 34.7 %collective-permute-done.11 = bf16[256,512]{1,0:T(8,128)(2,1)S(1)} collective-permute-done((bf16[256,512]{1,0:T(8,128)(2,1)S(1)}, bf16[256,512]{1,0:T(8,128)(2,1)S(1)}, u32[]{:S(2)}, u32[]{:S(2)}) %collective-permute-start.11) | collective-permute-done | bytes 262176 | tf_op jit(solution)/shard_map/ppermute | solution.py:17
  906.3 2.7 add_convert_fusion
  (335 shorter events, 182.9 us)
Async XLA Ops:
  6.5 305.8 %all-gather.2.cloned.1.call-start = ((), (), s32[]{:S(2)}) async-start(), calls=%async_computation | async-start | bytes 3727360 | tf_op jit(solution)/shard_map/all_gather | solution.py:75
  8.7 312.1 %copy-start.2 = (bf16[1024,512]{1,0:T(8,128)(2,1)S(1)}, bf16[1024,512]{1,0:T(8,128)(2,1)}, u32[]{:S(2)}) copy-start(bf16[1024,512]{1,0:T(8,128)(2,1)} %param.21) | copy-start | bytes 3145732
  315.0 10.9 %collective-permute-start = (bf16[256,512]{1,0:T(8,128)(2,1)S(1)}, bf16[256,512]{1,0:T(8,128)(2,1)S(1)}, u32[]{:S(2)}, u32[]{:S(2)}) collective-permute-start(bf16[256,512]{1,0:T(8,128)(2,1)S(1)} %bitcast.205), channel_id=1, source_target_pairs={{0,1},{1,2},{2,3},{3,4},{4,5},{5,6},{6,7},{7,8},{8,9},{9,10},{10,1... | collective-permute-start | bytes 786440 | tf_op jit(solution)/shard_map/ppermute | solution.py:14
  318.9 7.7 collective-permute-start.1
  323.9 4.2 copy-start.5
  323.9 4.2 copy-start.6
  485.5 1.6 copy-start.1
  489.2 2.1 copy-start.3
  491.4 11.5 %copy-start.4 = (bf16[1024,512]{1,0:T(8,128)(2,1)S(1)}, bf16[1024,512]{1,0:T(8,128)(2,1)}, u32[]{:S(2)}) copy-start(bf16[1024,512]{1,0:T(8,128)(2,1)} %copy-done.3) | copy-start | bytes 3145732
  492.0 13.9 %collective-permute-start.2 = (bf16[256,512]{1,0:T(8,128)(2,1)S(1)}, bf16[256,512]{1,0:T(8,128)(2,1)S(1)}, u32[]{:S(2)}, u32[]{:S(2)}) collective-permute-start(bf16[256,512]{1,0:T(8,128)(2,1)S(1)} %bitcast.206), channel_id=1, source_target_pairs={{0,1},{1,2},{2,3},{3,4},{4,5},{5,6},{6,7},{7,8},{8,9},{9,10},{10,1... | collective-permute-start | bytes 786440 | tf_op jit(solution)/shard_map/ppermute | solution.py:14
  500.9 11.2 %collective-permute-start.3 = (bf16[256,512]{1,0:T(8,128)(2,1)S(1)}, bf16[256,512]{1,0:T(8,128)(2,1)S(1)}, u32[]{:S(2)}, u32[]{:S(2)}) collective-permute-start(bf16[256,512]{1,0:T(8,128)(2,1)S(1)} %bitcast.204), channel_id=1, source_target_pairs={{1,0},{2,1},{3,2},{4,3},{5,4},{6,5},{7,6},{8,7},{9,8},{10,9},{11,1... | collective-permute-start | bytes 786440 | tf_op jit(solution)/shard_map/ppermute | solution.py:17
  662.9 1.6 copy-start
  664.5 2.3 copy-start.9
  703.6 7.1 collective-permute-start.4
  705.9 9.0 collective-permute-start.5
  715.0 21.6 %copy-start.7 = (s32[6]{0:T(128)S(1)}, s32[6]{0:T(128)}, u32[]{:S(2)}) copy-start(s32[6]{0:T(128)} %param.29) | copy-start | bytes 76
  715.0 21.6 %copy-start.8 = (s32[6]{0:T(128)S(1)}, s32[6]{0:T(128)}, u32[]{:S(2)}) copy-start(s32[6]{0:T(128)} %param.30) | copy-start | bytes 76
  716.4 13.8 %collective-permute-start.6 = (bf16[256,512]{1,0:T(8,128)(2,1)S(1)}, bf16[256,512]{1,0:T(8,128)(2,1)S(1)}, u32[]{:S(2)}, u32[]{:S(2)}) collective-permute-start(bf16[256,512]{1,0:T(8,128)(2,1)S(1)} %convolution_convert_fusion.3), channel_id=1, source_target_pairs={{0,1},{1,2},{2,3},{3,4},{4,5},{5,6},{6,7},{7,8},{8,9},{9,10},{10,1... | collective-permute-start | bytes 786440 | tf_op jit(solution)/shard_map/ppermute | solution.py:14
  726.9 9.6 %collective-permute-start.7 = (bf16[256,512]{1,0:T(8,128)(2,1)S(1)}, bf16[256,512]{1,0:T(8,128)(2,1)S(1)}, u32[]{:S(2)}, u32[]{:S(2)}) collective-permute-start(bf16[256,512]{1,0:T(8,128)(2,1)S(1)} %convolution_convert_fusion.3), channel_id=1, source_target_pairs={{1,0},{2,1},{3,2},{4,3},{5,4},{6,5},{7,6},{8,7},{9,8},{10,9},{11,1... | collective-permute-start | bytes 786440 | tf_op jit(solution)/shard_map/ppermute | solution.py:17
  774.8 7.4 collective-permute-start.8
  777.5 8.4 collective-permute-start.9
  822.8 48.1 %collective-permute-start.10 = (bf16[256,512]{1,0:T(8,128)(2,1)S(1)}, bf16[256,512]{1,0:T(8,128)(2,1)S(1)}, u32[]{:S(2)}, u32[]{:S(2)}) collective-permute-start(bf16[256,512]{1,0:T(8,128)(2,1)S(1)} %add_convert_fusion.3), channel_id=1, source_target_pairs={{0,1},{1,2},{2,3},{3,4},{4,5},{5,6},{6,7},{7,8},{8,9},{9,10},{10,1... | collective-permute-start | bytes 786440 | tf_op jit(solution)/shard_map/ppermute | solution.py:14
  867.6 38.0 %collective-permute-start.11 = (bf16[256,512]{1,0:T(8,128)(2,1)S(1)}, bf16[256,512]{1,0:T(8,128)(2,1)S(1)}, u32[]{:S(2)}, u32[]{:S(2)}) collective-permute-start(bf16[256,512]{1,0:T(8,128)(2,1)S(1)} %add_convert_fusion.3), channel_id=1, source_target_pairs={{1,0},{2,1},{3,2},{4,3},{5,4},{6,5},{7,6},{8,7},{9,8},{10,9},{11,1... | collective-permute-start | bytes 786440 | tf_op jit(solution)/shard_map/ppermute | solution.py:17
Sparse Core Ops, SparseCore 0:
  9.4 302.8 all-gather.1
where the time goes:
time: 922 us; the launch traced here: 916 us
  waiting for transfers between devices  366 us (40%)
  loops' own time  253 us (27%)
  local copies, waits for them, and re-layouts  91.8 us (10%)
  matrix products  89.6 us (10%)
  starting transfers between devices  86.3 us (9%)
  other arithmetic  15.4 us (2%)
  between operations  13.9 us (2%)
    all_gather x1, waiting for transfers between devices, on_device(): matrices = lax.all_gather(weights, 'dom', axis=1, tiled=True)  304 us
    another operation x4, loops' own time, aggregate(): total = lax.fori_loop(0, tiles.shape[0], add_tile, total)  237 us
    ppermute x6, starting transfers between devices, with_halo(): lax.ppermute(lax.slice_in_dim(block, block.shape[dim] - width, None, axis...  73.1 us
    dot_general x60, matrix products, add_tile(): message = jnp.dot(tile, block, preferred_element_type=jnp.float32)  64.1 us
    ppermute x6, waiting for transfers between devices, with_halo(): lax.ppermute(lax.slice_in_dim(block, 0, width, axis=dim), axis, backward)  55.7 us
    dynamic_slice x120, local copies, waits for them, and re-layouts, add_tile(): current = lax.dynamic_index_in_dim(total, target[index], 0, keepdims=False)  38.6 us
    dynamic_slice x60, local copies, waits for them, and re-layouts, add_tile(): block = lax.dynamic_index_in_dim(proj_all, source[index], 0, keepdims=False)  37.4 us
  transfers between devices with their start and end apart: 13, of which 11 were waited for; matrix products, arithmetic and copies ran while one was open for 1% of the time, Pallas kernels for 0%

commit v1 on v0

v1 whole, which is shorter than its diff:
```python
import jax
import jax.numpy as jnp
from jax import lax
from jax.experimental import pallas as pl
from jax.experimental.pallas import tpu as pltpu
from jax.sharding import Mesh, PartitionSpec as P

E = 128
NB = 8
HB = 2
NC = 2
W = 512
HALF = 256
SPLIT = ("zh", "core", "y", "x", "zl")
CHAIN = ("zh", "core", "y", "x", "zl")
DOM = ("y", "x", "zl")
F32 = jnp.float32
BF16 = jnp.bfloat16
VMEM = pl.BlockSpec(memory_space=pltpu.VMEM)
SMEM = pl.BlockSpec(memory_space=pltpu.SMEM)


def shape(rows, dtype=BF16):
    return jax.ShapeDtypeStruct((rows, W), dtype)


def call(body, outs, specs, scratch, flops, data):
    return pl.pallas_call(
        body,
        out_shape=outs,
        in_specs=specs,
        out_specs=[VMEM] * len(outs),
        scratch_shapes=scratch,
        compiler_params=pltpu.CompilerParams(vmem_limit_bytes=40 * 1024 * 1024),
        cost_estimate=pl.CostEstimate(flops=flops, bytes_accessed=data, transcendentals=0),
    )


def rows_at(index, count=E):
    return pl.ds(pl.multiple_of(index * E, E), count)


def dot(a, b):
    return jnp.dot(a, b, preferred_element_type=F32)


def silu(v):
    half = 0.5 * v
    return half + half * jnp.tanh(half)


def add_tiles(tiles, target, source, blocks, total):
    total[...] = jnp.zeros_like(total)
    for t in range(tiles.shape[0]):
        total[rows_at(target[t]), :] += dot(tiles[t], blocks[rows_at(source[t]), :])


def place(core, mine, other, index, full):
    piece = mine[:, index].reshape(W, HALF)
    full[:, pl.ds(pl.multiple_of(core * HALF, HALF), HALF)] = piece
    piece = other[:, index].reshape(W, HALF)
    full[:, pl.ds(pl.multiple_of((1 - core) * HALF, HALF), HALF)] = piece


def first_sums(target, source, halo, nodes, before, after, tiles, summed, left, right, blocks, total):
    blocks[: NB * E, :] = nodes[...]
    blocks[NB * E : (NB + HB) * E, :] = before[...]
    blocks[(NB + HB) * E :, :] = after[...]
    add_tiles(tiles, target, source, blocks, total)
    summed[...] = total[...].astype(BF16)
    for k in range(HB):
        left[k * E : (k + 1) * E, :] = summed[rows_at(halo[k]), :]
        right[k * E : (k + 1) * E, :] = summed[rows_at(halo[HB + k]), :]


def step_rows(blocks, sums, own, near, out, start, count):
    at = slice(start, start + count)
    old = blocks[at, :]
    mixed = dot(old, own[...]) + dot(sums[at, :], near[...])
    out[at, :] = (old.astype(F32) + silu(mixed)).astype(BF16)


def fine_rounds(
    core, target, source, pooled, nodes, before, after, summed, sum_before, sum_after, tiles, mine, other, scale,
    skip, left, middle, right,
    blocks, sums, total, message, own, near, both, shares,
):
    place(core[0], mine, other, 0, message)
    place(core[0], mine, other, 1, own)
    place(core[0], mine, other, 2, near)
    both[...] = dot(message[...], near[...]).astype(BF16)
    blocks[: NB * E, :] = nodes[...]
    blocks[NB * E : (NB + HB) * E, :] = before[...]
    blocks[(NB + HB) * E :, :] = after[...]
    sums[: NB * E, :] = summed[...]
    sums[NB * E : (NB + HB) * E, :] = sum_before[...]
    sums[(NB + HB) * E :, :] = sum_after[...]
    for start in range(0, (NB + 2 * HB) * E, 256):
        step_rows(blocks, sums, own, both, blocks, start, 256)
    add_tiles(tiles, target, source, blocks, total)
    sums[: NB * E, :] = total[...].astype(BF16)
    for start in range(0, NB * E, 256):
        step_rows(blocks, sums, own, both, skip, start, 256)
    factors = scale[...].T
    shares[...] = jnp.zeros_like(shares)
    for f in range(NB):
        block = skip[f * E : (f + 1) * E, :].astype(F32)
        shares[rows_at(pooled[f]), :] += block * factors[:, f : f + 1]
    left[...] = shares[: NC * E, :].astype(BF16)
    middle[...] = shares[NC * E : 2 * NC * E, :]
    right[...] = shares[2 * NC * E :, :].astype(BF16)


def join_coarse(core, mine, other, own, both, lift, message, near):
    place(core[0], mine, other, 0, message)
    place(core[0], mine, other, 1, own)
    place(core[0], mine, other, 2, near)
    place(core[0], mine, other, 3, lift)
    both[...] = dot(message[...], near[...]).astype(BF16)


def coarse_round(target, source, state, before, after, tiles, own, both, out, blocks, total):
    blocks[: NC * E, :] = before[...]
    blocks[NC * E : 2 * NC * E, :] = state[...]
    blocks[2 * NC * E :, :] = after[...]
    add_tiles(tiles, target, source, blocks, total)
    old = state[...]
    mixed = dot(old, own[...]) + dot(total[...].astype(BF16), both[...])
    out[...] = (old.astype(F32) + silu(mixed)).astype(BF16)


def lift_back(pooled, skip, state, before, after, lift, out, lifted):
    lifted[: NC * E, :] = dot(before[...], lift[...])
    lifted[NC * E : 2 * NC * E, :] = dot(state[...], lift[...])
    lifted[2 * NC * E :, :] = dot(after[...], lift[...])
    for f in range(NB):
        at = slice(f * E, (f + 1) * E)
        out[at, :] = (skip[at, :].astype(F32) + lifted[rows_at(pooled[f]), :]).astype(BF16)


def exchange(to_before, to_after, axes):
    count = 1
    for axis in axes:
        count *= lax.axis_size(axis)
    up = [(i, i + 1) for i in range(count - 1)]
    down = [(b, a) for a, b in up]
    return lax.ppermute(to_after, axes, up), lax.ppermute(to_before, axes, down)


def spread(piece, axes):
    count = 1
    for axis in axes:
        count *= lax.axis_size(axis)
    return lax.all_to_all(jnp.broadcast_to(piece[None], (count,) + piece.shape), axes, 0, 0)


def on_device(
    nodes,
    fine_tiles,
    fine_target,
    fine_source,
    halo_ids,
    pool_map,
    pool_weight,
    coarse_tiles,
    coarse_target,
    coarse_source,
    weights,
):
    core = lax.axis_index("core").astype(jnp.int32)
    halo = halo_ids.reshape(-1)
    blocks = nodes.reshape(NB, E, W)
    to_before = blocks[halo[:HB]].reshape(-1, W)
    to_after = blocks[halo[HB:]].reshape(-1, W)
    before, after = exchange(to_before, to_after, CHAIN)

    half = lax.dynamic_slice_in_dim(weights, core * HALF, HALF, axis=2)
    column = spread(half, ("zl",)).transpose(1, 0, 2, 3).reshape(7, -1, HALF)
    fine_mine = spread(column[:3], ("y", "x"))
    fine_other = lax.ppermute(fine_mine, "core", [(0, 1), (1, 0)])

    tile_bytes = 2 * fine_tiles.size
    summed, sums_left, sums_right = call(
        first_sums,
        [shape(NB * E), shape(HB * E), shape(HB * E)],
        [SMEM] * 3 + [VMEM] * 4,
        [pltpu.VMEM(((NB + 2 * HB) * E, W), BF16), pltpu.VMEM((NB * E, W), F32)],
        2 * 24 * E * E * W,
        tile_bytes + 3 * NB * E * W,
    )(fine_target, fine_source, halo, nodes, before, after, fine_tiles)
    sum_before, sum_after = exchange(sums_left, sums_right, CHAIN)

    coarse_mine = spread(column[3:], ("y", "x"))
    coarse_other = lax.ppermute(coarse_mine, "core", [(0, 1), (1, 0)])

    square = pltpu.VMEM((W, W), BF16)
    skip, left, middle, right = call(
        fine_rounds,
        [shape(NB * E), shape(NC * E), shape(NC * E, F32), shape(NC * E)],
        [SMEM] * 4 + [VMEM] * 10,
        [
            pltpu.VMEM(((NB + 2 * HB) * E, W), BF16),
            pltpu.VMEM(((NB + 2 * HB) * E, W), BF16),
            pltpu.VMEM((NB * E, W), F32),
            square,
            square,
            square,
            square,
            pltpu.VMEM((3 * NC * E, W), F32),
        ],
        2 * 24 * E * E * W + 2 * 5 * NB * E * W * W,
        tile_bytes + 8 * NB * E * W,
    )(
        core.reshape(1),
        fine_target,
        fine_source,
        pool_map,
        nodes,
        before,
        after,
        summed,
        sum_before,
        sum_after,
        fine_tiles,
        fine_mine,
        fine_other,
        pool_weight.reshape(NB, E).astype(F32),
    )
    from_before, from_after = exchange(left, right, DOM)
    state = (middle + from_before.astype(F32) + from_after.astype(F32)).astype(BF16)

    own, both, lift = call(
        join_coarse,
        [shape(W), shape(W), shape(W)],
        [SMEM] + [VMEM] * 2,
        [square, square],
        2 * W * W * W,
        8 * 2 * W * W,
    )(core.reshape(1), coarse_mine, coarse_other)
    for turn in range(2):
        near = exchange(state, state, DOM)
        (state,) = call(
            coarse_round,
            [shape(NC * E)],
            [SMEM] * 2 + [VMEM] * 6,
            [pltpu.VMEM((3 * NC * E, W), BF16), pltpu.VMEM((NC * E, W), F32)],
            2 * 6 * E * E * W + 4 * NC * E * W * W,
            2 * coarse_tiles.size + 4 * W * W,
        )(coarse_target, coarse_source, state, *near, coarse_tiles, own, both)
    near = exchange(state, state, DOM)
    (result,) = call(
        lift_back,
        [shape(NB * E)],
        [SMEM] + [VMEM] * 5,
        [pltpu.VMEM((3 * NC * E, W), F32)],
        2 * 3 * NC * E * W * W,
        4 * NB * E * W,
    )(pool_map, skip, state, *near, lift)
    return result


def solution(mesh):
    fine = Mesh(mesh.devices.reshape(4, 2, 4, 4, 4), SPLIT)
    return jax.shard_map(
        on_device,
        mesh=fine,
        in_specs=(
            P(SPLIT, None),
            P(SPLIT, None, None),
            P(SPLIT),
            P(SPLIT),
            P(SPLIT, None, None),
            P(SPLIT),
            P(SPLIT),
            P(SPLIT, None, None),
            P(SPLIT),
            P(SPLIT),
            P(None, DOM, None),
        ),
        out_specs=P(SPLIT, None),
        check_vma=False,
    )
```

time: 922 us -> 173 us (0.19)
  the two profiles are of different devices: /device:TPU:187 before, /device:TPU:1 now
where the time goes in v1:
time: 173 us; the launch traced here: 172 us
  waiting for transfers between devices  76.5 us (44%)
  starting transfers between devices  57.1 us (33%)
  Pallas kernels  15.3 us (9%)
  local copies, waits for them, and re-layouts  11.3 us (7%)
  blocking collectives  11 us (6%)
    ppermute x6, waiting for transfers between devices, exchange(): lax.ppermute(to_before, axes, down)  50.2 us
    ppermute x6, starting transfers between devices, exchange(): lax.ppermute(to_before, axes, down)  23.3 us
    ppermute x6, starting transfers between devices, exchange(): lax.ppermute(to_after, axes, up)  16.2 us
    ppermute x6, waiting for transfers between devices, exchange(): lax.ppermute(to_after, axes, up)  14.2 us
    all_to_all x2, waiting for transfers between devices, spread(): lax.all_to_all(jnp.broadcast_to(piece[None], (count,) + piece.shape), axe...  12.1 us
    all_to_all x1, blocking collectives, spread(): lax.all_to_all(jnp.broadcast_to(piece[None], (count,) + piece.shape), axe...  11 us
    all_to_all x2, starting transfers between devices, spread(): lax.all_to_all(jnp.broadcast_to(piece[None], (count,) + piece.shape), axe...  10.6 us
    pallas_call x1, Pallas kernels, on_device(): call(fine_rounds, [shape(NB * E), shape(NC * E), shape(NC * E, F32), shap...  6.89 us
  transfers between devices with their start and end apart: 16, of which 13 were waited for; matrix products, arithmetic and copies ran while one was open for 2% of the time, Pallas kernels for 6%

profile of v1, /device:TPU:1, one launch (start us, length us, event | category | flops | bytes accessed | tf_op | source)
XLA Modules:
  0.0 171.7 jit_solution(693502498374309502)
XLA Ops:
  0.8 11.0 %all_to_all.15 = bf16[4,7,8,256]{3,2,1,0:T(8,128)(2,1)S(1)} all-to-all(bf16[4,7,8,256]{3,2,1,0:T(8,128)(2,1)S(1)} %broadcast_in_dim.10), channel_id=1, replica_groups=mesh['zh'=4,'core'=2,'y'=4,'x'=4,'zl'=4] {'zl'}, dimensions={0} | all-to-all | bytes 229376 | tf_op jit(solution)/shard_map/all_to_all | solution.py:154
  12.8 6.8 %all-to-all-start.1 = ((bf16[16,3,32,256]{3,2,1,0:T(8,128)(2,1)}), bf16[16,3,32,256]{3,2,1,0:T(8,128)(2,1)S(1)}, u32[]{:S(2)}, u32[]{:S(2)}) async-start(bf16[16,3,32,256]{3,2,1,0:T(8,128)(2,1)} %broadcast_in_dim.12), calls=%async_computation.1 | async-start | bytes 1572864 | tf_op jit(solution)/shard_map/all_to_all | solution.py:154
  19.6 12.1 %all-to-all-done.1.mine = bf16[16,3,32,256]{3,2,1,0:T(8,128)(2,1)S(1)} async-done(((bf16[16,3,32,256]{3,2,1,0:T(8,128)(2,1)}), bf16[16,3,32,256]{3,2,1,0:T(8,128)(2,1)S(1)}, u32[]{:S(2)}, u32[]{:S(2)}) %all-to-all-start.1) | async-done | bytes 786464 | tf_op jit(solution)/shard_map/all_to_all | solution.py:154
  32.8 3.8 %all-to-all-start.2 = ((bf16[16,4,32,256]{3,2,1,0:T(8,128)(2,1)}), bf16[16,4,32,256]{3,2,1,0:T(8,128)(2,1)S(1)}, u32[]{:S(2)}, u32[]{:S(2)}) async-start(bf16[16,4,32,256]{3,2,1,0:T(8,128)(2,1)} %broadcast_in_dim.28), calls=%async_computation.2 | async-start | bytes 2097152 | tf_op jit(solution)/shard_map/all_to_all | solution.py:154
  36.6 5.2 %collective-permute-start.4 = (bf16[16,3,32,256]{3,2,1,0:T(8,128)(2,1)S(1)}, bf16[16,3,32,256]{3,2,1,0:T(8,128)(2,1)}, u32[]{:S(2)}, u32[]{:S(2)}) collective-permute-start(bf16[16,3,32,256]{3,2,1,0:T(8,128)(2,1)S(1)} %all-to-all-done.1.mine), channel_id=1, source_target_pairs={{0,64},{64,0},{1,65},{65,1},{2,66},{66,2},{3,67},{67,3},{4,68},{68... | collective-permute-start | bytes 2359304 | tf_op jit(solution)/shard_map/ppermute | solution.py:180
  43.1 2.9 %collective-permute-start = (bf16[256,512]{1,0:T(8,128)(2,1)}, bf16[256,512]{1,0:T(8,128)(2,1)S(1)}, u32[]{:S(2)}, u32[]{:S(2)}) collective-permute-start(bf16[256,512]{1,0:T(8,128)(2,1)} %bitcast.4), channel_id=1, source_target_pairs={{0,1},{1,2},{2,3},{3,4},{4,5},{5,6},{6,7},{7,8},{8,9},{9,10},{10,1... | collective-permute-start | bytes 786440 | tf_op jit(solution)/shard_map/ppermute | solution.py:147
  47.3 8.8 %collective-permute-start.1 = (bf16[256,512]{1,0:T(8,128)(2,1)}, bf16[256,512]{1,0:T(8,128)(2,1)S(1)}, u32[]{:S(2)}, u32[]{:S(2)}) collective-permute-start(bf16[256,512]{1,0:T(8,128)(2,1)} %bitcast.26), channel_id=1, source_target_pairs={{1,0},{2,1},{3,2},{4,3},{5,4},{6,5},{7,6},{8,7},{9,8},{10,9},{11,1... | collective-permute-start | bytes 786440 | tf_op jit(solution)/shard_map/ppermute | solution.py:147
  57.4 4.7 %collective-permute-done.1.after = bf16[256,512]{1,0:T(8,128)(2,1)S(1)} collective-permute-done((bf16[256,512]{1,0:T(8,128)(2,1)}, bf16[256,512]{1,0:T(8,128)(2,1)S(1)}, u32[]{:S(2)}, u32[]{:S(2)}) %collective-permute-start.1) | collective-permute-done | bytes 262176 | tf_op jit(solution)/shard_map/ppermute | solution.py:147
  63.2 2.6 %shard_map.109 = (bf16[1024,512]{1,0:T(8,128)(2,1)S(1)}, bf16[256,512]{1,0:T(8,128)(2,1)}, bf16[256,512]{1,0:T(8,128)(2,1)}) custom-call(s32[24]{0:T(128)S(1)} %copy-done.7, s32[24]{0:T(128)S(1)} %copy-done.8, s32[4]{0:T(128)S(1)} %reshape.89.halo, bf16[1024,512]{1,0:T(8,128)(2,1)S(1)} %copy-done.1, bf16[256,512]{1,0:T(8,128)(2,1)S(1)} %collective-permute-done.before, ...), custom_call_target="tpu_custom_call" | custom-call | flops 402653184 | bytes 2359296 | tf_op jit(solution)/shard_map/pallas_call | solution.py:183
  66.8 2.3 %collective-permute-start.2 = (bf16[256,512]{1,0:T(8,128)(2,1)}, bf16[256,512]{1,0:T(8,128)(2,1)}, u32[]{:S(2)}, u32[]{:S(2)}) collective-permute-start(bf16[256,512]{1,0:T(8,128)(2,1)} %get-tuple-element.16), channel_id=1, source_target_pairs={{0,1},{1,2},{2,3},{3,4},{4,5},{5,6},{6,7},{7,8},{8,9},{9,10},{10,1... | collective-permute-start | bytes 786440 | tf_op jit(solution)/shard_map/ppermute | solution.py:147
  69.2 9.4 %collective-permute-start.3 = (bf16[256,512]{1,0:T(8,128)(2,1)}, bf16[256,512]{1,0:T(8,128)(2,1)}, u32[]{:S(2)}, u32[]{:S(2)}) collective-permute-start(bf16[256,512]{1,0:T(8,128)(2,1)} %get-tuple-element.17), channel_id=1, source_target_pairs={{1,0},{2,1},{3,2},{4,3},{5,4},{6,5},{7,6},{8,7},{9,8},{10,9},{11,1... | collective-permute-start | bytes 786440 | tf_op jit(solution)/shard_map/ppermute | solution.py:147
  78.5 1.9 %collective-permute-start.9 = (bf16[16,4,32,256]{3,2,1,0:T(8,128)(2,1)S(1)}, bf16[16,4,32,256]{3,2,1,0:T(8,128)(2,1)S(1)}, u32[]{:S(2)}, u32[]{:S(2)}) collective-permute-start(bf16[16,4,32,256]{3,2,1,0:T(8,128)(2,1)S(1)} %all-to-all-done.2.mine), channel_id=1, source_target_pairs={{0,64},{64,0},{1,65},{65,1},{2,66},{66,2},{3,67},{67,3},{4,68},{68... | collective-permute-start | bytes 3145736 | tf_op jit(solution)/shard_map/ppermute | solution.py:194
  81.1 3.5 %collective-permute-done.3.sum_after = bf16[256,512]{1,0:T(8,128)(2,1)} collective-permute-done((bf16[256,512]{1,0:T(8,128)(2,1)}, bf16[256,512]{1,0:T(8,128)(2,1)}, u32[]{:S(2)}, u32[]{:S(2)}) %collective-permute-start.3) | collective-permute-done | bytes 262176 | tf_op jit(solution)/shard_map/ppermute | solution.py:147
  87.6 6.9 %shard_map.110 = (bf16[1024,512]{1,0:T(8,128)(2,1)S(1)}, bf16[256,512]{1,0:T(8,128)(2,1)S(1)}, f32[256,512]{1,0:T(8,128)S(1)}, bf16[256,512]{1,0:T(8,128)(2,1)S(1)}) custom-call(s32[1]{0:T(128)} %bitcast.core, s32[24]{0:T(128)S(1)} %copy-done.7, s32[24]{0:T(128)S(1)} %copy-done.8, s32[8]{0:T(128)S(1)} %copy-done.9, bf16[1024,512]{1,0:T(8,128)(2,1)S(1)} %copy-done.1, ...), custom_call_target="tpu_custom_call" | custom-call | flops 3087007744 | bytes 4980736 | tf_op jit(solution)/shard_map/pallas_call | solution.py:197
  94.5 1.8 %collective-permute-start.5 = (bf16[256,512]{1,0:T(8,128)(2,1)S(1)}, bf16[256,512]{1,0:T(8,128)(2,1)S(1)}, u32[]{:S(2)}, u32[]{:S(2)}) collective-permute-start(bf16[256,512]{1,0:T(8,128)(2,1)S(1)} %get-tuple-element.20), channel_id=1, source_target_pairs={{0,1},{1,2},{2,3},{3,4},{4,5},{5,6},{6,7},{7,8},{8,9},{9,10},{10,1... | collective-permute-start | bytes 786440 | tf_op jit(solution)/shard_map/ppermute | solution.py:147
  96.3 1.3 collective-permute-start.6
  97.6 3.0 %collective-permute-done.5 = bf16[256,512]{1,0:T(8,128)(2,1)S(1)} collective-permute-done((bf16[256,512]{1,0:T(8,128)(2,1)S(1)}, bf16[256,512]{1,0:T(8,128)(2,1)S(1)}, u32[]{:S(2)}, u32[]{:S(2)}) %collective-permute-start.5) | collective-permute-done | bytes 262176 | tf_op jit(solution)/shard_map/ppermute | solution.py:147
  100.6 10.0 %collective-permute-done.6 = bf16[256,512]{1,0:T(8,128)(2,1)S(1)} collective-permute-done((bf16[256,512]{1,0:T(8,128)(2,1)S(1)}, bf16[256,512]{1,0:T(8,128)(2,1)S(1)}, u32[]{:S(2)}, u32[]{:S(2)}) %collective-permute-start.6) | collective-permute-done | bytes 262176 | tf_op jit(solution)/shard_map/ppermute | solution.py:147
  110.7 3.7 %collective-permute-start.7 = (bf16[256,512]{1,0:T(8,128)(2,1)S(1)}, bf16[256,512]{1,0:T(8,128)(2,1)S(1)}, u32[]{:S(2)}, u32[]{:S(2)}) collective-permute-start(bf16[256,512]{1,0:T(8,128)(2,1)S(1)} %add_convert_fusion.state), channel_id=1, source_target_pairs={{0,1},{1,2},{2,3},{3,4},{4,5},{5,6},{6,7},{7,8},{8,9},{9,10},{10,1... | collective-permute-start | bytes 786440 | tf_op jit(solution)/shard_map/ppermute | solution.py:147
  114.5 1.3 collective-permute-start.8
  116.3 2.5 %collective-permute-done.7.before = bf16[256,512]{1,0:T(8,128)(2,1)S(1)} collective-permute-done((bf16[256,512]{1,0:T(8,128)(2,1)S(1)}, bf16[256,512]{1,0:T(8,128)(2,1)S(1)}, u32[]{:S(2)}, u32[]{:S(2)}) %collective-permute-start.7) | collective-permute-done | bytes 262176 | tf_op jit(solution)/shard_map/ppermute | solution.py:147
  118.8 10.4 %collective-permute-done.8.after = bf16[256,512]{1,0:T(8,128)(2,1)S(1)} collective-permute-done((bf16[256,512]{1,0:T(8,128)(2,1)S(1)}, bf16[256,512]{1,0:T(8,128)(2,1)S(1)}, u32[]{:S(2)}, u32[]{:S(2)}) %collective-permute-start.8) | collective-permute-done | bytes 262176 | tf_op jit(solution)/shard_map/ppermute | solution.py:147
  129.9 1.5 shard_map.112.state
  131.3 2.9 %collective-permute-start.10 = (bf16[256,512]{1,0:T(8,128)(2,1)S(1)}, bf16[256,512]{1,0:T(8,128)(2,1)S(1)}, u32[]{:S(2)}, u32[]{:S(2)}) collective-permute-start(bf16[256,512]{1,0:T(8,128)(2,1)S(1)} %shard_map.112.state), channel_id=1, source_target_pairs={{0,1},{1,2},{2,3},{3,4},{4,5},{5,6},{6,7},{7,8},{8,9},{9,10},{10,1... | collective-permute-start | bytes 786440 | tf_op jit(solution)/shard_map/ppermute | solution.py:147
  134.3 1.3 collective-permute-start.11
  135.6 3.2 %collective-permute-done.10.before = bf16[256,512]{1,0:T(8,128)(2,1)S(1)} collective-permute-done((bf16[256,512]{1,0:T(8,128)(2,1)S(1)}, bf16[256,512]{1,0:T(8,128)(2,1)S(1)}, u32[]{:S(2)}, u32[]{:S(2)}) %collective-permute-start.10) | collective-permute-done | bytes 262176 | tf_op jit(solution)/shard_map/ppermute | solution.py:147
  138.7 10.9 %collective-permute-done.11.after = bf16[256,512]{1,0:T(8,128)(2,1)S(1)} collective-permute-done((bf16[256,512]{1,0:T(8,128)(2,1)S(1)}, bf16[256,512]{1,0:T(8,128)(2,1)S(1)}, u32[]{:S(2)}, u32[]{:S(2)}) %collective-permute-start.11) | collective-permute-done | bytes 262176 | tf_op jit(solution)/shard_map/ppermute | solution.py:147
  149.7 1.4 shard_map.113.state
  151.1 2.6 %collective-permute-start.12 = (bf16[256,512]{1,0:T(8,128)(2,1)S(1)}, bf16[256,512]{1,0:T(8,128)(2,1)S(1)}, u32[]{:S(2)}, u32[]{:S(2)}) collective-permute-start(bf16[256,512]{1,0:T(8,128)(2,1)S(1)} %shard_map.113.state), channel_id=1, source_target_pairs={{0,1},{1,2},{2,3},{3,4},{4,5},{5,6},{6,7},{7,8},{8,9},{9,10},{10,1... | collective-permute-start | bytes 786440 | tf_op jit(solution)/shard_map/ppermute | solution.py:147
  155.0 3.7 %collective-permute-done.12.before = bf16[256,512]{1,0:T(8,128)(2,1)S(1)} collective-permute-done((bf16[256,512]{1,0:T(8,128)(2,1)S(1)}, bf16[256,512]{1,0:T(8,128)(2,1)S(1)}, u32[]{:S(2)}, u32[]{:S(2)}) %collective-permute-start.12) | collective-permute-done | bytes 262176 | tf_op jit(solution)/shard_map/ppermute | solution.py:147
  158.7 10.6 %collective-permute-done.13.after = bf16[256,512]{1,0:T(8,128)(2,1)S(1)} collective-permute-done((bf16[256,512]{1,0:T(8,128)(2,1)S(1)}, bf16[256,512]{1,0:T(8,128)(2,1)S(1)}, u32[]{:S(2)}, u32[]{:S(2)}) %collective-permute-start.13) | collective-permute-done | bytes 262176 | tf_op jit(solution)/shard_map/ppermute | solution.py:147
  169.4 2.4 %shard_map.114 = bf16[1024,512]{1,0:T(8,128)(2,1)} custom-call(s32[8]{0:T(128)S(1)} %copy-done.9, bf16[1024,512]{1,0:T(8,128)(2,1)S(1)} %get-tuple-element.18.skip, bf16[256,512]{1,0:T(8,128)(2,1)S(1)} %shard_map.113.state, bf16[256,512]{1,0:T(8,128)(2,1)S(1)} %collective-permute-done.12.before, bf16[256,512]{1,0:T(8,128)(2,1)S(1)} %collective-permute-done.13.after, ...), custom_call_target="tpu_custom_call" | custom-call | flops 402653184 | bytes 2097152 | tf_op jit(solution)/shard_map/pallas_call | solution.py:251
  (49 shorter events, 15.1 us)
Async XLA Ops:
  0.0 0.8 copy-start
  12.8 18.9 %all-to-all-start.1 = ((bf16[16,3,32,256]{3,2,1,0:T(8,128)(2,1)}), bf16[16,3,32,256]{3,2,1,0:T(8,128)(2,1)S(1)}, u32[]{:S(2)}, u32[]{:S(2)}) async-start(bf16[16,3,32,256]{3,2,1,0:T(8,128)(2,1)} %broadcast_in_dim.12), calls=%async_computation.1 | async-start | bytes 1572864 | tf_op jit(solution)/shard_map/all_to_all | solution.py:154
  32.8 9.0 %copy-start.13 = (s32[1,2,2]{2,1,0:T(2,128)S(1)}, s32[1,2,2]{2,1,0:T(2,128)}, u32[]{:S(2)}) copy-start(s32[1,2,2]{2,1,0:T(2,128)} %param.15) | copy-start | bytes 52
  32.8 9.0 %copy-start.1 = (bf16[1024,512]{1,0:T(8,128)(2,1)S(1)}, bf16[1024,512]{1,0:T(8,128)(2,1)}, u32[]{:S(2)}) copy-start(bf16[1024,512]{1,0:T(8,128)(2,1)} %nodes.3) | copy-start | bytes 3145732
  32.8 45.7 %all-to-all-start.2 = ((bf16[16,4,32,256]{3,2,1,0:T(8,128)(2,1)}), bf16[16,4,32,256]{3,2,1,0:T(8,128)(2,1)S(1)}, u32[]{:S(2)}, u32[]{:S(2)}) async-start(bf16[16,4,32,256]{3,2,1,0:T(8,128)(2,1)} %broadcast_in_dim.28), calls=%async_computation.2 | async-start | bytes 2097152 | tf_op jit(solution)/shard_map/all_to_all | solution.py:154
  36.6 48.0 %collective-permute-start.4 = (bf16[16,3,32,256]{3,2,1,0:T(8,128)(2,1)S(1)}, bf16[16,3,32,256]{3,2,1,0:T(8,128)(2,1)}, u32[]{:S(2)}, u32[]{:S(2)}) collective-permute-start(bf16[16,3,32,256]{3,2,1,0:T(8,128)(2,1)S(1)} %all-to-all-done.1.mine), channel_id=1, source_target_pairs={{0,64},{64,0},{1,65},{65,1},{2,66},{66,2},{3,67},{67,3},{4,68},{68... | collective-permute-start | bytes 2359304 | tf_op jit(solution)/shard_map/ppermute | solution.py:180
  43.1 14.2 %collective-permute-start = (bf16[256,512]{1,0:T(8,128)(2,1)}, bf16[256,512]{1,0:T(8,128)(2,1)S(1)}, u32[]{:S(2)}, u32[]{:S(2)}) collective-permute-start(bf16[256,512]{1,0:T(8,128)(2,1)} %bitcast.4), channel_id=1, source_target_pairs={{0,1},{1,2},{2,3},{3,4},{4,5},{5,6},{6,7},{7,8},{8,9},{9,10},{10,1... | collective-permute-start | bytes 786440 | tf_op jit(solution)/shard_map/ppermute | solution.py:147
  47.2 14.8 %copy-start.7 = (s32[24]{0:T(128)S(1)}, s32[24]{0:T(128)}, u32[]{:S(2)}) copy-start(s32[24]{0:T(128)} %target.5) | copy-start | bytes 292
  47.3 14.8 %copy-start.8 = (s32[24]{0:T(128)S(1)}, s32[24]{0:T(128)}, u32[]{:S(2)}) copy-start(s32[24]{0:T(128)} %source.5) | copy-start | bytes 292
  47.3 14.8 %collective-permute-start.1 = (bf16[256,512]{1,0:T(8,128)(2,1)}, bf16[256,512]{1,0:T(8,128)(2,1)S(1)}, u32[]{:S(2)}, u32[]{:S(2)}) collective-permute-start(bf16[256,512]{1,0:T(8,128)(2,1)} %bitcast.26), channel_id=1, source_target_pairs={{1,0},{2,1},{3,2},{4,3},{5,4},{6,5},{7,6},{8,7},{9,8},{10,9},{11,1... | collective-permute-start | bytes 786440 | tf_op jit(solution)/shard_map/ppermute | solution.py:147
  62.1 1.1 copy-start.3
  65.8 1.0 copy-start.10
  66.8 13.7 %copy-start.12 = (bf16[1024]{0:T(1024)(128)(2,1)S(1)}, bf16[1024]{0:T(1024)(128)(2,1)}, u32[]{:S(2)}) copy-start(bf16[1024]{0:T(1024)(128)(2,1)} %param.17) | copy-start | bytes 6148
  66.8 14.3 %collective-permute-start.2 = (bf16[256,512]{1,0:T(8,128)(2,1)}, bf16[256,512]{1,0:T(8,128)(2,1)}, u32[]{:S(2)}, u32[]{:S(2)}) collective-permute-start(bf16[256,512]{1,0:T(8,128)(2,1)} %get-tuple-element.16), channel_id=1, source_target_pairs={{0,1},{1,2},{2,3},{3,4},{4,5},{5,6},{6,7},{7,8},{8,9},{9,10},{10,1... | collective-permute-start | bytes 786440 | tf_op jit(solution)/shard_map/ppermute | solution.py:147
  69.2 15.5 %collective-permute-start.3 = (bf16[256,512]{1,0:T(8,128)(2,1)}, bf16[256,512]{1,0:T(8,128)(2,1)}, u32[]{:S(2)}, u32[]{:S(2)}) collective-permute-start(bf16[256,512]{1,0:T(8,128)(2,1)} %get-tuple-element.17), channel_id=1, source_target_pairs={{1,0},{2,1},{3,2},{4,3},{5,4},{6,5},{7,6},{8,7},{9,8},{10,9},{11,1... | collective-permute-start | bytes 786440 | tf_op jit(solution)/shard_map/ppermute | solution.py:147
  78.5 37.2 %collective-permute-start.9 = (bf16[16,4,32,256]{3,2,1,0:T(8,128)(2,1)S(1)}, bf16[16,4,32,256]{3,2,1,0:T(8,128)(2,1)S(1)}, u32[]{:S(2)}, u32[]{:S(2)}) collective-permute-start(bf16[16,4,32,256]{3,2,1,0:T(8,128)(2,1)S(1)} %all-to-all-done.2.mine), channel_id=1, source_target_pairs={{0,64},{64,0},{1,65},{65,1},{2,66},{66,2},{3,67},{67,3},{4,68},{68... | collective-permute-start | bytes 3145736 | tf_op jit(solution)/shard_map/ppermute | solution.py:194
  84.6 0.7 copy-start.9
  85.3 1.1 copy-start.4
  86.4 1.2 copy-start.11
  94.5 6.0 %collective-permute-start.5 = (bf16[256,512]{1,0:T(8,128)(2,1)S(1)}, bf16[256,512]{1,0:T(8,128)(2,1)S(1)}, u32[]{:S(2)}, u32[]{:S(2)}) collective-permute-start(bf16[256,512]{1,0:T(8,128)(2,1)S(1)} %get-tuple-element.20), channel_id=1, source_target_pairs={{0,1},{1,2},{2,3},{3,4},{4,5},{5,6},{6,7},{7,8},{8,9},{9,10},{10,1... | collective-permute-start | bytes 786440 | tf_op jit(solution)/shard_map/ppermute | solution.py:147
  96.3 14.3 %collective-permute-start.6 = (bf16[256,512]{1,0:T(8,128)(2,1)S(1)}, bf16[256,512]{1,0:T(8,128)(2,1)S(1)}, u32[]{:S(2)}, u32[]{:S(2)}) collective-permute-start(bf16[256,512]{1,0:T(8,128)(2,1)S(1)} %get-tuple-element.21), channel_id=1, source_target_pairs={{1,0},{2,1},{3,2},{4,3},{5,4},{6,5},{7,6},{8,7},{9,8},{10,9},{11,1... | collective-permute-start | bytes 786440 | tf_op jit(solution)/shard_map/ppermute | solution.py:147
  110.7 18.5 %copy-start.2 = (bf16[6,128,128]{2,1,0:T(8,128)(2,1)S(1)}, bf16[6,128,128]{2,1,0:T(8,128)(2,1)}, u32[]{:S(2)}) copy-start(bf16[6,128,128]{2,1,0:T(8,128)(2,1)} %tiles.7) | copy-start | bytes 589828
  110.7 8.1 %collective-permute-start.7 = (bf16[256,512]{1,0:T(8,128)(2,1)S(1)}, bf16[256,512]{1,0:T(8,128)(2,1)S(1)}, u32[]{:S(2)}, u32[]{:S(2)}) collective-permute-start(bf16[256,512]{1,0:T(8,128)(2,1)S(1)} %add_convert_fusion.state), channel_id=1, source_target_pairs={{0,1},{1,2},{2,3},{3,4},{4,5},{5,6},{6,7},{7,8},{8,9},{9,10},{10,1... | collective-permute-start | bytes 786440 | tf_op jit(solution)/shard_map/ppermute | solution.py:147
  114.5 14.8 %collective-permute-start.8 = (bf16[256,512]{1,0:T(8,128)(2,1)S(1)}, bf16[256,512]{1,0:T(8,128)(2,1)S(1)}, u32[]{:S(2)}, u32[]{:S(2)}) collective-permute-start(bf16[256,512]{1,0:T(8,128)(2,1)S(1)} %add_convert_fusion.state), channel_id=1, source_target_pairs={{1,0},{2,1},{3,2},{4,3},{5,4},{6,5},{7,6},{8,7},{9,8},{10,9},{11,1... | collective-permute-start | bytes 786440 | tf_op jit(solution)/shard_map/ppermute | solution.py:147
  129.2 0.7 copy-start.5
  129.2 0.7 copy-start.6
  131.3 7.4 %collective-permute-start.10 = (bf16[256,512]{1,0:T(8,128)(2,1)S(1)}, bf16[256,512]{1,0:T(8,128)(2,1)S(1)}, u32[]{:S(2)}, u32[]{:S(2)}) collective-permute-start(bf16[256,512]{1,0:T(8,128)(2,1)S(1)} %shard_map.112.state), channel_id=1, source_target_pairs={{0,1},{1,2},{2,3},{3,4},{4,5},{5,6},{6,7},{7,8},{8,9},{9,10},{10,1... | collective-permute-start | bytes 786440 | tf_op jit(solution)/shard_map/ppermute | solution.py:147
  134.3 15.4 %collective-permute-start.11 = (bf16[256,512]{1,0:T(8,128)(2,1)S(1)}, bf16[256,512]{1,0:T(8,128)(2,1)S(1)}, u32[]{:S(2)}, u32[]{:S(2)}) collective-permute-start(bf16[256,512]{1,0:T(8,128)(2,1)S(1)} %shard_map.112.state), channel_id=1, source_target_pairs={{1,0},{2,1},{3,2},{4,3},{5,4},{6,5},{7,6},{8,7},{9,8},{10,9},{11,1... | collective-permute-start | bytes 786440 | tf_op jit(solution)/shard_map/ppermute | solution.py:147
  151.1 7.6 %collective-permute-start.12 = (bf16[256,512]{1,0:T(8,128)(2,1)S(1)}, bf16[256,512]{1,0:T(8,128)(2,1)S(1)}, u32[]{:S(2)}, u32[]{:S(2)}) collective-permute-start(bf16[256,512]{1,0:T(8,128)(2,1)S(1)} %shard_map.113.state), channel_id=1, source_target_pairs={{0,1},{1,2},{2,3},{3,4},{4,5},{5,6},{6,7},{7,8},{8,9},{9,10},{10,1... | collective-permute-start | bytes 786440 | tf_op jit(solution)/shard_map/ppermute | solution.py:147
  153.7 15.7 %collective-permute-start.13 = (bf16[256,512]{1,0:T(8,128)(2,1)S(1)}, bf16[256,512]{1,0:T(8,128)(2,1)S(1)}, u32[]{:S(2)}, u32[]{:S(2)}) collective-permute-start(bf16[256,512]{1,0:T(8,128)(2,1)S(1)} %shard_map.113.state), channel_id=1, source_target_pairs={{1,0},{2,1},{3,2},{4,3},{5,4},{6,5},{7,6},{8,7},{9,8},{10,9},{11,1... | collective-permute-start | bytes 786440 | tf_op jit(solution)/shard_map/ppermute | solution.py:147
